TPU v7x, 32 devices: a whole 2x2x4 slice. The times are simulated.
32 devices in a mesh: dp: 8 (over z, y), mp: 4 (over x, core).
Axes of the slice: x: 2, y: 2, z: 4, core: 2. Of those that a mesh axis runs over, the one named last changes fastest.
Arguments:
- hidden: bfloat16 [2048, 8192], P('dp', 'mp'), may hold values from -6 to 6
- target_gain: float32 [8192], replicated, may hold values from 0.1 to 1.9
- target_weight: bfloat16 [2048, 8192], P('mp'), may hold values from -0.0625 to 0.0625
- draft_gain: float32 [8192], P('mp'), may hold values from 0.1 to 1.9
- draft_weight: bfloat16 [2048, 8192], P('dp', 'mp'), may hold values from -0.0625 to 0.0625
- logits: bfloat16 [2048, 32000], P('dp', 'mp'), may hold values from -40 to 300
- seq_lens: int32 [8, 2], P('dp'), may hold values from 32 to 128, as said below
- tool_mask: int32 [2048], P('dp'), may hold values 0 or 1
- owners: int32 [2048, 1], P('dp'), may hold values from 0 to 7; in each aligned block of 256 rows (0 to 255, 256 to 511, ...) at most 40 rows name the same one
Outputs:
- grad_weight: float32 [2048, 8192], P('dp', 'mp')
- grad_gain: float32 [8192], P('mp')
- slot_loss: float32 [2560], P('dp')
Inputs may be any that keep to these rules, and one draw needn't show every extreme that they name: `owners`: in the rows of one index of dp at most 40 name the same owner, a bound that some block reaches. `seq_lens`: in each index of dp some sequence has length exactly 128.
All inputs are finite; a program needn't handle non-finite values. No bound on the sum of `tool_mask` on one device may be relied on, other than what follows from the above.
Results may differ from a plain program's by a relative error of at most 0.0085.
Values may be sent and summed in bfloat16 or wider, within the bound.
A program may use at most 128 MiB of HBM per device.

v0:
```python
import math

import jax
import jax.numpy as jnp
from jax import lax
from jax.sharding import PartitionSpec as P

VOCAB = 32000
LEN = 128
SEQS = 2


EPSILON = 1e-05


def joined(shard, axis, combine):
    everything = jax.tree.map(lambda part: lax.all_gather(part, axis), shard)
    leading = jax.tree.map(lambda part: part[0], everything)

    def step(k, so_far):
        return combine(so_far, jax.tree.map(lambda part: part[k], everything))

    return lax.fori_loop(1, lax.axis_size(axis), step, leading)


def vocab_weight(logit_rows, valid_rows):
    values = logit_rows.astype(jnp.float32)
    highest = jnp.max(values, axis=1)
    shifted = values - highest[:, None]
    expsum = jnp.exp(shifted)
    total = jnp.sum(expsum, axis=1)
    moment = jnp.sum(expsum * shifted, axis=1)

    def combine(first, second):
        peak = jnp.maximum(first[0], second[0])
        left_factor = jnp.exp(first[0] - peak)
        right_factor = jnp.exp(second[0] - peak)
        total_sum = first[1] * left_factor + second[1] * right_factor
        moment_sum = left_factor * (first[2] + (first[0] - peak) * first[1]) + right_factor * (
            second[2] + (second[0] - peak) * second[1]
        )
        return (peak, total_sum, moment_sum)

    highest, total, moment = joined((highest, total, moment), "mp", combine)
    entropy = jnp.log(total) - moment / total
    return (valid_rows * entropy / math.log(VOCAB)).astype(jnp.bfloat16)


def on_device(
    hidden,
    target_gain,
    target_weight,
    draft_gain,
    draft_weight,
    logits,
    seq_lens,
    tool_mask,
    owners,
):
    token_rows = hidden.shape[0]
    local_width = hidden.shape[1]
    group_count = lax.axis_size("dp")
    model_count = lax.axis_size("mp")
    capacity = max(2, 5 * token_rows // (4 * group_count))
    slot_rows = group_count * capacity
    hidden_float = hidden.astype(jnp.float32)
    squares = lax.psum(jnp.sum(hidden_float * hidden_float, axis=1), "mp")
    inverse = lax.rsqrt(squares / (local_width * model_count) + EPSILON)
    normed_piece = (
        lax.all_gather(hidden, "mp", axis=1, tiled=True).astype(jnp.float32)
        * inverse[:, None]
        * target_gain
    ).astype(jnp.bfloat16)
    teacher = lax.dot_general(
        normed_piece, target_weight, (((1,), (1,)), ((), ())), preferred_element_type=jnp.float32
    ).astype(jnp.bfloat16)
    row_index = jnp.arange(token_rows, dtype=jnp.int32)
    position = row_index % LEN
    sequence = row_index // LEN
    lookup = sequence[:, None] == jnp.arange(SEQS, dtype=jnp.int32)[None, :]
    length = jnp.sum(jnp.where(lookup, seq_lens[0][None, :], 0), axis=1)
    valid = jnp.logical_and(position < length - 1, tool_mask == 1).astype(jnp.float32)
    owner = owners[:, 0]
    member = (owner[:, None] == jnp.arange(group_count, dtype=jnp.int32)[None, :]).astype(jnp.int32)
    running = jnp.cumsum(member, axis=0)
    rank = jnp.sum(running * member, axis=1) - 1
    slot_of_row = owner * capacity + rank
    select_mask = slot_of_row[None, :] == jnp.arange(slot_rows, dtype=jnp.int32)[:, None]
    weight = vocab_weight(logits, valid).astype(jnp.float32)
    normed = (hidden_float * inverse[:, None] * draft_gain).astype(jnp.bfloat16)
    full_weight = lax.all_gather(draft_weight, "dp", axis=0, tiled=True)
    partial_value = lax.dot_general(
        normed, full_weight, (((1,), (1,)), ((), ())), preferred_element_type=jnp.float32
    )
    projection = lax.psum(partial_value, "mp")
    teacher_full = lax.all_gather(teacher, "mp", axis=1, tiled=True)
    error = projection - teacher_full.astype(jnp.float32)
    scale = 1.0 / math.sqrt(token_rows * group_count)
    grad_out = (weight[:, None] * error * scale).astype(jnp.bfloat16)
    row_loss = 0.5 * weight * jnp.sum(error * error, axis=1) * scale
    grad_weight = lax.psum_scatter(
        lax.dot_general(
            grad_out, normed, (((0,), (0,)), ((), ())), preferred_element_type=jnp.float32
        ),
        "dp",
        scatter_dimension=0,
        tiled=True,
    )
    grad_normed = jnp.dot(grad_out, full_weight, preferred_element_type=jnp.float32)
    gain_local = jnp.sum(grad_normed * hidden_float * inverse[:, None], axis=0)
    grad_gain = lax.psum(gain_local, "dp")
    select_float = select_mask.astype(jnp.float32)
    packed_loss = jnp.dot(select_float, row_loss[:, None], precision=lax.Precision.HIGHEST)
    packed_loss = packed_loss.reshape(group_count, capacity)
    row_loss = lax.all_to_all(packed_loss, "dp", split_axis=0, concat_axis=0, tiled=True).reshape(
        slot_rows
    )
    return (grad_weight, grad_gain, row_loss)


def solution(mesh):
    in_specs = (
        P("dp", "mp"),
        P(),
        P("mp", None),
        P("mp"),
        P("dp", "mp"),
        P("dp", "mp"),
        P("dp", None),
        P("dp"),
        P("dp", None),
    )
    out_specs = (P("dp", "mp"), P("mp"), P("dp"))
    return jax.shard_map(
        on_device, mesh=mesh, in_specs=in_specs, out_specs=out_specs, check_vma=False
    )
```

profile of v0, /device:TPU:0, one launch (start us, length us, event | category | flops | bytes accessed | tf_op | source)
XLA Modules:
  0.0 545.6 jit_solution(18181016494568716242)
XLA Ops:
  7.2 0.7 all-gather.12.cloned.1.call-update
  8.0 0.7 all-gather.10.cloned.1.call-update
  8.7 0.3 fusion.5
  9.0 8.3 %psum.21 = f32[256]{0:T(256)S(1)} all-reduce(f32[256]{0:T(256)S(1)} %fusion.5), channel_id=1, replica_groups=mesh['dp'=8,'mp'=4] {'mp'}, use_global_device_ids=true, to_apply=%region_7.8 | all-reduce | flops 256 | bytes 2048 | tf_op jit(solution)/shard_map/psum | solution.py:67
  17.4 29.4 %all-gather.12.cloned.1.call-done = bf16[256,8192]{1,0:T(8,128)(2,1)} async-done(((bf16[256,2048]{1,0:T(8,128)(2,1)}), bf16[256,8192]{1,0:T(8,128)(2,1)}) %all-gather.12.cloned.1.call-update) | async-done | bytes 4194320 | tf_op jit(solution)/shard_map/all_gather | solution.py:70
  46.8 7.7 %fusion.9 = bf16[256,512]{1,0:T(8,128)(2,1)} fusion(bf16[512,8192]{1,0:T(8,128)(2,1)} %param.13, bf16[256,8192]{1,0:T(8,128)(2,1)} %all-gather.12.cloned.1.call-done, f32[8192]{0:T(1024)S(1)} %copy-done.10, f32[256]{0:T(256)S(1)} %add_rsqrt_fusion), kind=kOutput, calls=%fused_computation.24 | convolution fusion | flops 2156003328 | bytes 12878848 | tf_op jit(solution)/shard_map/dot_general | solution.py:74
  54.6 3.6 reduce_max.18
  58.2 4.4 fusion
  62.6 5.1 all-gather.4
  67.7 5.1 all-gather.5
  72.7 5.1 all-gather.3
  77.8 96.1 %all-gather.10.cloned.1.call-done = bf16[2048,2048]{1,0:T(8,128)(2,1)} async-done(((bf16[256,2048]{1,0:T(8,128)(2,1)}), bf16[2048,2048]{1,0:T(8,128)(2,1)}) %all-gather.10.cloned.1.call-update) | async-done | bytes 8388624 | tf_op jit(solution)/shard_map/all_gather | solution.py:91
  173.9 7.1 %fusion.13 = f32[256,2048]{1,0:T(8,128)} fusion(bf16[2048,2048]{1,0:T(8,128)(2,1)} %all-gather.10.cloned.1.call-done, bf16[256,2048]{1,0:T(8,128)(2,1)S(1)} %copy-done, f32[2048]{0:T(1024)S(1)} %copy-done.7, f32[256]{0:T(256)S(1)} %add_rsqrt_fusion), kind=kOutput, calls=%fused_computation.28 | convolution fusion | flops 2149580800 | bytes 11543552 | tf_op jit(solution)/shard_map/dot_general | solution.py:92
  181.1 0.2 reduce-scatter.2.cloned.1.call-start
  181.3 0.4 slice-done
  181.7 0.3 while.19
  182.1 8.3 %all-gather.14.cloned.1.call-done = bf16[256,2048]{1,0:T(8,128)(2,1)} async-done(((bf16[256,512]{1,0:T(8,128)(2,1)}), bf16[256,2048]{1,0:T(8,128)(2,1)}) %all-gather.14.cloned.1.call-update) | async-done | bytes 1048592 | tf_op jit(solution)/shard_map/all_gather | solution.py:96
  190.4 54.2 %all-reduce.2.cloned.1.call-done = f32[256,2048]{1,0:T(8,128)} async-done(((f32[256,2048]{1,0:T(8,128)}), f32[256,2048]{1,0:T(8,128)}) %all-reduce.2.cloned.1.call-update) | async-done | bytes 2097168 | tf_op jit(solution)/shard_map/psum | solution.py:95
  244.6 2.4 multiply_reduce_fusion
  247.1 0.4 multiply_convert_fusion.2
  247.5 8.2 %fusion.11 = f32[2048,2048]{1,0:T(8,128)} fusion(bf16[256,2048]{1,0:T(8,128)(2,1)S(1)} %multiply_convert_fusion.2, bf16[256,2048]{1,0:T(8,128)(2,1)S(1)} %copy-done, f32[2048]{0:T(1024)S(1)} %copy-done.7, f32[256]{0:T(256)S(1)} %add_rsqrt_fusion), kind=kOutput, calls=%fused_computation.27 | convolution fusion | flops 2149580800 | bytes 18883584 | tf_op jit(solution)/shard_map/dot_general | solution.py:102
  255.8 0.7 copy-done.6
  256.4 0.6 reduce-window.6
  257.0 0.2 slice_reduce_fusion
  257.3 1.1 convolution_bitcast_fusion
  258.4 5.5 %all-to-all-start = ((f32[8,1,40]{2,1,0:T(1,128)}), f32[8,1,40]{2,1,0:T(1,128)S(1)}, u32[]{:S(2)}, u32[]{:S(2)}) async-start(f32[8,1,40]{2,1,0:T(1,128)} %convolution_bitcast_fusion), calls=%async_computation.1 | async-start | bytes 8192 | tf_op jit(solution)/shard_map/all_to_all | solution.py:115
  263.9 5.8 %fusion.8 = f32[2048]{0:T(1024)S(1)} fusion(bf16[256,2048]{1,0:T(8,128)(2,1)S(1)} %copy-done, bf16[256,2048]{1,0:T(8,128)(2,1)S(1)} %multiply_convert_fusion.2, bf16[2048,2048]{1,0:T(8,128)(2,1)} %all-gather.10.cloned.1.call-done, f32[256]{0:T(256)S(1)} %add_rsqrt_fusion), kind=kOutput, calls=%fused_computation.23 | convolution fusion | flops 2149578752 | bytes 10494976 | tf_op jit(solution)/shard_map/dot_general | solution.py:109
  269.7 24.3 %psum.23 = f32[2048]{0:T(1024)} all-reduce(f32[2048]{0:T(1024)S(1)} %fusion.8), channel_id=1, replica_groups=mesh['dp'=8,'mp'=4] {'dp'}, use_global_device_ids=true, to_apply=%region_11.12 | all-reduce | flops 2048 | bytes 16384 | tf_op jit(solution)/shard_map/psum | solution.py:111
  294.0 0.5 broadcast.106
  294.6 0.7 reduce.6
  295.2 0.7 reshape.90
  295.9 243.2 %reduce-scatter.2.cloned.1.call-done = f32[256,2048]{1,0:T(8,128)} async-done(((f32[2048,2048]{1,0:T(8,128)}), f32[256,2048]{1,0:T(8,128)}) %reduce-scatter.2.cloned.1.call-update) | async-done | bytes 2097168 | tf_op jit(solution)/shard_map/reduce_scatter | solution.py:101
  (63 shorter events, 0.8 us)
Async XLA Ops:
  7.2 1.6 copy-start
  7.2 39.6 %copy-start.10 = (f32[8192]{0:T(1024)S(1)}, f32[8192]{0:T(1024)}, u32[]{:S(2)}) copy-start(f32[8192]{0:T(1024)} %param.12) | copy-start | bytes 98308
  7.2 39.6 %all-gather.12.cloned.1.call-start = ((), (), s32[]{:S(2)}) async-start(), calls=%async_computation.4 | async-start | bytes 5242880 | tf_op jit(solution)/shard_map/all_gather | solution.py:70
  7.9 166.0 %all-gather.10.cloned.1.call-start = ((), (), s32[]{:S(2)}) async-start(), calls=%async_computation.2 | async-start | bytes 9437184 | tf_op jit(solution)/shard_map/all_gather | solution.py:91
  8.7 181.7 %all-gather.14.cloned.1.call-start = ((), (), s32[]{:S(2)}) async-start(), calls=%async_computation.5 | async-start | bytes 1310720 | tf_op jit(solution)/shard_map/all_gather | solution.py:96
  54.6 190.0 %all-reduce.2.cloned.1.call-start = ((), (), s32[]{:S(2)}) async-start(), calls=%async_computation.3 | async-start | bytes 4194304 | tf_op jit(solution)/shard_map/psum | solution.py:95
  58.2 115.7 %copy-start.7 = (f32[2048]{0:T(1024)S(1)}, f32[2048]{0:T(1024)}, u32[]{:S(2)}) copy-start(f32[2048]{0:T(1024)} %param.14) | copy-start | bytes 24580
  67.7 113.3 %copy-start.3 = (f32[4,1,256]{2,1,0:T(1,128)}, f32[4,1,256]{2,1,0:T(1,128)S(1)}, u32[]{:S(2)}) copy-start(f32[4,1,256]{2,1,0:T(1,128)S(1)} %all-gather.4) | copy-start | bytes 12292
  72.7 108.3 %copy-start.5 = (f32[4,1,256]{2,1,0:T(1,128)}, f32[4,1,256]{2,1,0:T(1,128)S(1)}, u32[]{:S(2)}) copy-start(f32[4,1,256]{2,1,0:T(1,128)S(1)} %all-gather.5) | copy-start | bytes 12292
  77.8 103.2 %copy-start.4 = (f32[4,1,256]{2,1,0:T(1,128)}, f32[4,1,256]{2,1,0:T(1,128)S(1)}, u32[]{:S(2)}) copy-start(f32[4,1,256]{2,1,0:T(1,128)S(1)} %all-gather.3) | copy-start | bytes 12292
  181.0 1.0 copy-start.9
  181.0 0.7 slice-start
  181.0 0.7 slice-start.1
  181.0 0.7 slice-start.2
  181.1 65.9 %copy-start.8 = (s32[256]{0:T(256)S(1)}, s32[256]{0:T(256)}, u32[]{:S(2)}) copy-start(s32[256]{0:T(256)} %param.18) | copy-start | bytes 3076
  181.1 358.0 %reduce-scatter.2.cloned.1.call-start = ((), (), s32[]{:S(2)}) async-start(), calls=%async_computation.6 | async-start | bytes 18874368 | tf_op jit(solution)/shard_map/reduce_scatter | solution.py:101
  190.4 56.6 %copy-start.2 = (bf16[256,2048]{1,0:T(8,128)(2,1)S(1)}, bf16[256,2048]{1,0:T(8,128)(2,1)}, u32[]{:S(2)}) copy-start(bf16[256,2048]{1,0:T(8,128)(2,1)} %all-gather.14.cloned.1.call-done) | copy-start | bytes 3145732
  244.6 2.5 copy-start.1
  255.7 0.7 copy-start.6
  258.4 35.6 %all-to-all-start = ((f32[8,1,40]{2,1,0:T(1,128)}), f32[8,1,40]{2,1,0:T(1,128)S(1)}, u32[]{:S(2)}, u32[]{:S(2)}) async-start(f32[8,1,40]{2,1,0:T(1,128)} %convolution_bitcast_fusion), calls=%async_computation.1 | async-start | bytes 8192 | tf_op jit(solution)/shard_map/all_to_all | solution.py:115
Sparse Core Ops, SparseCore 0:
  9.6 37.1 all-gather.11
  48.9 124.9 all-gather.9
  175.5 14.8 all-gather.13
  193.2 51.3 all-reduce.1
  255.9 283.1 reduce-scatter.1
where the time goes:
time: 546 us
  waiting for transfers between devices  433 us (79%)
  blocking collectives  47.9 us (9%)
  matrix products  29.8 us (5%)
  between operations  13.9 us (3%)
  other arithmetic  12.6 us (2%)
  starting transfers between devices  5.89 us (1%)
    reduce_scatter x1, waiting for transfers between devices, on_device(): lax.psum_scatter(lax.dot_general(grad_out, normed, (((0,), (0,)), ((), ()...  243 us
    all_gather x1, waiting for transfers between devices, on_device(): full_weight = lax.all_gather(draft_weight, 'dp', axis=0, tiled=True)  96.1 us
    psum x1, waiting for transfers between devices, on_device(): projection = lax.psum(partial_value, 'mp')  54.2 us
    all_gather x1, waiting for transfers between devices, on_device(): lax.all_gather(hidden, 'mp', axis=1, tiled=True).astype(jnp.float32)  29.4 us
    psum x1, blocking collectives, on_device(): grad_gain = lax.psum(gain_local, 'dp')  24.3 us
    all_gather x3, blocking collectives, joined(): everything = jax.tree.map(lambda part: lax.all_gather(part, axis), shard)  15.2 us
  transfers between devices with their start and end apart: 6, of which 5 were waited for; matrix products, arithmetic and copies ran while one was open for 6% of the time, Pallas kernels for 0%

commit v1 on v0

v1 whole, which is shorter than its diff:
```python
import functools
import math

import jax
import jax.numpy as jnp
from jax import lax
from jax.experimental import pallas as pl
from jax.experimental.pallas import tpu as pltpu
from jax.sharding import PartitionSpec as P

LEN = 128
SEQS = 2
EPSILON = 1e-05
MESH = pl.DeviceIdType.MESH
F32 = jnp.float32
BF16 = jnp.bfloat16


def place_of(index, n):
    odd = lax.rem(index, 2)
    half = lax.div(index, 2)
    return (1 - odd) * half + odd * (n - 1 - half)


def index_of(place, n):
    late = lax.div(place, n // 2)
    return (1 - late) * (2 * place) + late * (2 * (n - 1 - place) + 1)


def kernel(
    n, k,
    hidden, tw, dw, logits, gd, gt, info,
    gw, gain_out, loss_out, msg_out,
    hid, lbuf, twb, wd, sbuf, st, smsg, cmsg, qf, gf,
    local_sem, ring_send, ring_recv, tw_send, tw_recv, ex_send, ex_recv,
    st_send, st_recv, c_send, c_recv, q_send, q_recv, g_send, g_recv,
):
    rows, width = hidden.shape
    kvb = dw.shape[0]
    half = rows // 2
    vocab = logits.shape[1] * k
    d = lax.axis_index("dp")
    m = lax.axis_index("mp")
    place = place_of(d, n)
    right = index_of(lax.rem(place + 1, n), n)
    left = index_of(lax.rem(place + n - 1, n), n)
    holder = lax.div(d * k, n)
    offset = pl.multiple_of(d * kvb - holder * tw.shape[0], 16)

    own_hidden = pltpu.make_async_copy(hidden, hid.at[0], local_sem.at[0])
    own_logits = pltpu.make_async_copy(logits, lbuf, local_sem.at[1])
    own_hidden.start()
    own_logits.start()

    barrier = pltpu.get_barrier_semaphore()
    for j in range(1, n):
        pl.semaphore_signal(
            barrier, inc=1, device_id={"dp": lax.rem(d + j, n)}, device_id_type=MESH
        )
    for j in range(1, k):
        pl.semaphore_signal(
            barrier, inc=1, device_id={"mp": lax.rem(m + j, k)}, device_id_type=MESH
        )
    pl.semaphore_wait(barrier, n - 1 + k - 1)

    def ring(way, t, h, first=False):
        part = pl.ds(h * half, half)
        if way == 0:
            source, target, to = t - 1, t, right
        else:
            source, target, to = lax.rem(n - t + 1, n), n - t, left
        return pltpu.make_async_remote_copy(
            src_ref=hidden.at[part] if first else hid.at[source, part],
            dst_ref=hid.at[target, part],
            send_sem=ring_send.at[way, t, h],
            recv_sem=ring_recv.at[way, t, h],
            device_id={"dp": to},
            device_id_type=MESH,
        )

    for h in (0, 1):
        for way in (0, 1):
            ring(way, 1, h if way == 0 else 1 - h, True).start()

    def tw_columns(index):
        return tw.at[pl.ds(offset, kvb), pl.ds(pl.multiple_of(index * width, width), width)]

    def tw_copy(j):
        to = lax.rem(m + j, k)
        return pltpu.make_async_remote_copy(
            src_ref=tw_columns(to), dst_ref=twb,
            send_sem=tw_send.at[j], recv_sem=tw_recv,
            device_id={"mp": to}, device_id_type=MESH,
        )

    tw_own = pltpu.make_async_copy(tw_columns(m), twb, local_sem.at[2])

    @pl.when(m == holder)
    def _():
        for j in range(1, k):
            tw_copy(j).start()
        tw_own.start()

    own_hidden.wait()
    own_logits.wait()

    def row_stats(i, carry):
        r = pl.ds(pl.multiple_of(i * 16, 16), 16)
        values = lbuf[r, :].astype(F32)
        highest = jnp.max(values, axis=1, keepdims=True)
        shifted = values - highest
        expsum = jnp.exp(shifted)
        total = jnp.sum(expsum, axis=1, keepdims=True)
        moment = jnp.sum(expsum * shifted, axis=1, keepdims=True)
        features = hid[0, r, :].astype(F32)
        squares = jnp.sum(features * features, axis=1, keepdims=True)
        lane = lax.broadcasted_iota(jnp.int32, (16, 128), 1)
        st[r, :] = jnp.where(
            lane == 0, highest, jnp.where(lane == 1, total, jnp.where(lane == 2, moment, squares))
        )
        return carry

    lax.fori_loop(0, rows // 16, row_stats, 0)
    smsg[m] = st[...].T[0:8, :]

    def st_copy(j):
        return pltpu.make_async_remote_copy(
            src_ref=smsg.at[m], dst_ref=smsg.at[m],
            send_sem=st_send.at[j], recv_sem=st_recv.at[j],
            device_id={"mp": lax.rem(m + j, k)}, device_id_type=MESH,
        )

    for j in range(1, k):
        st_copy(j).start()
    for j in range(1, k):
        st_copy(j).wait()
    highest = smsg[0, 0:1, :]
    for j in range(1, k):
        highest = jnp.maximum(highest, smsg[j, 0:1, :])
    total = jnp.zeros_like(highest)
    moment = jnp.zeros_like(highest)
    squares = jnp.zeros_like(highest)
    for j in range(k):
        below = smsg[j, 0:1, :] - highest
        factor = jnp.exp(below)
        total += factor * smsg[j, 1:2, :]
        moment += factor * (smsg[j, 2:3, :] + below * smsg[j, 1:2, :])
        squares += smsg[j, 3:4, :]
    inverse = lax.rsqrt(squares / (width * k) + EPSILON)
    entropy = jnp.log(total) - moment / total
    weight = (info[0:1, :] * entropy / math.log(vocab)).astype(BF16).astype(F32)
    factor = weight * inverse * inverse * (1.0 / math.sqrt(rows * n))
    line = lax.broadcasted_iota(jnp.int32, (8, rows), 0)
    cmsg[d] = jnp.where(line == 0, factor, info[1:2, :])

    def c_copy(j):
        return pltpu.make_async_remote_copy(
            src_ref=cmsg.at[d], dst_ref=cmsg.at[d],
            send_sem=c_send.at[j], recv_sem=c_recv.at[j],
            device_id={"dp": lax.rem(d + j, n)}, device_id_type=MESH,
        )

    for j in range(1, n):
        c_copy(j).start()
    gw[...] = jnp.zeros_like(gw)

    def arrive(t, last, onward):
        for h in (0, 1):
            for way in (0, 1):
                part = h if way == 0 else 1 - h
                if last and h == 1:
                    continue
                ring(way, t, part).wait_recv()
                if h == 0:
                    if onward:
                        ring(way, t + 1, part).start()
                elif onward:
                    @pl.when(t + 1 < n // 2)
                    def _():
                        ring(way, t + 1, part).start()

    arrive(1, n == 2, n > 2)

    @pl.when(m == holder)
    def _():
        tw_own.wait()
        for j in range(1, k):
            tw_copy(j).wait_send()

    @pl.when(m != holder)
    def _():
        tw_copy(1).wait_recv()

    gt_part = gt[:, pl.ds(pl.multiple_of(m * width, width), width)]

    def blend(i, carry):
        r = pl.ds(pl.multiple_of(i * 16, 16), 16)
        wd[r, :] = (
            gd[...] * dw[r, :].astype(F32) - gt_part * twb[r, :].astype(F32)
        ).astype(BF16)
        return carry

    lax.fori_loop(0, kvb // 16, blend, 0)

    def exchange(s, j):
        return pltpu.make_async_remote_copy(
            src_ref=sbuf.at[s, m], dst_ref=sbuf.at[s, m],
            send_sem=ex_send.at[s, j], recv_sem=ex_recv.at[s, j],
            device_id={"mp": lax.rem(m + j, k)}, device_id_type=MESH,
        )

    def project(s):
        sbuf[s, m] = lax.dot_general(
            hid[s], wd[...], (((1,), (1,)), ((), ())), preferred_element_type=F32
        ).astype(BF16)
        for j in range(1, k):
            exchange(s, j).start()

    piece = min(width, 512)

    def consume(s):
        for j in range(1, k):
            exchange(s, j).wait()
        total = sbuf[s, 0].astype(F32)
        for j in range(1, k):
            total += sbuf[s, j].astype(F32)
        block = index_of(lax.rem(place - s + n, n), n)
        factor = jnp.broadcast_to(cmsg[block][0:1, :], (128, rows)).T[:, 0:1]
        grad = (total * factor).astype(BF16)
        squares = lax.dot_general(
            jnp.ones((8, kvb), F32), total * total, (((1,), (1,)), ((), ())),
            precision=lax.Precision.HIGHEST, preferred_element_type=F32,
        )
        qf[d, block] = squares[0:1, :]
        for c in range(0, width, piece):
            gw[:, c:c + piece] += lax.dot_general(
                grad, hid[s, :, c:c + piece], (((0,), (0,)), ((), ())),
                preferred_element_type=F32,
            )

    project(0)
    for j in range(1, n):
        c_copy(j).wait()

    def step(t, carry):
        project(t)
        project(n - t)

        @pl.when(t + 1 < n // 2)
        def _():
            arrive(t + 1, False, True)

        @pl.when(t + 1 == n // 2)
        def _():
            arrive(n // 2, True, False)

        @pl.when(t == 1)
        def _():
            consume(0)

        @pl.when(t > 1)
        def _():
            consume(t - 1)
            consume(n - t + 1)

        return carry

    lax.fori_loop(1, n // 2, step, 0)
    project(n // 2)
    consume(n // 2 - 1)
    consume(n // 2 + 1)
    consume(n // 2)

    gf[d] = jnp.sum(dw[...].astype(F32) * gw[...], axis=0, keepdims=True)

    def q_copy(j):
        return pltpu.make_async_remote_copy(
            src_ref=qf.at[d], dst_ref=qf.at[d],
            send_sem=q_send.at[j], recv_sem=q_recv.at[j],
            device_id={"dp": lax.rem(d + j, n)}, device_id_type=MESH,
        )

    def g_copy(j):
        return pltpu.make_async_remote_copy(
            src_ref=gf.at[d], dst_ref=gf.at[d],
            send_sem=g_send.at[j], recv_sem=g_recv.at[j],
            device_id={"dp": lax.rem(d + j, n)}, device_id_type=MESH,
        )

    for j in range(1, n):
        q_copy(j).start()
        g_copy(j).start()
    msg_out[...] = cmsg[...]

    def sent(t, carry):
        for way in (0, 1):
            ring(way, t, way).wait_send()

            @pl.when(t < n // 2)
            def _():
                ring(way, t, 1 - way).wait_send()

        return carry

    for way in (0, 1):
        for h in (0, 1):
            ring(way, 1, h, True).wait_send()
    lax.fori_loop(2, n // 2 + 1, sent, 0)
    for j in range(1, n):
        q_copy(j).wait()
        g_copy(j).wait()
    gain = gf[0]
    loss = qf[0]
    for j in range(1, n):
        gain += gf[j]
        loss += qf[j]
    gain_out[...] = gain
    for j in range(n):
        loss_out[j] = loss[j] * (0.5 * cmsg[j, 0:1, :])


def on_device(
    hidden, target_gain, target_weight, draft_gain, draft_weight, logits, seq_lens, tool_mask, owners
):
    n = lax.axis_size("dp")
    k = lax.axis_size("mp")
    rows, width = hidden.shape
    kvb = draft_weight.shape[0]
    capacity = max(2, 5 * rows // (4 * n))
    index = jnp.arange(rows, dtype=jnp.int32)
    position = index % LEN
    lookup = (index // LEN)[:, None] == jnp.arange(SEQS, dtype=jnp.int32)[None, :]
    length = jnp.sum(jnp.where(lookup, seq_lens[0][None, :], 0), axis=1)
    valid = jnp.logical_and(position < length - 1, tool_mask == 1).astype(F32)
    info = jnp.stack([valid, owners[:, 0].astype(F32)])
    anywhere = pl.BlockSpec(memory_space=pl.ANY)
    vmem = pl.BlockSpec(memory_space=pltpu.VMEM)
    dma = pltpu.SemaphoreType.DMA
    gw, gain, loss, messages = pl.pallas_call(
        functools.partial(kernel, n, k),
        out_shape=(
            jax.ShapeDtypeStruct((kvb, width), F32),
            jax.ShapeDtypeStruct((1, width), F32),
            jax.ShapeDtypeStruct((n, 1, rows), F32),
            jax.ShapeDtypeStruct((n, 8, rows), F32),
        ),
        in_specs=[anywhere, anywhere, vmem, anywhere, vmem, vmem, vmem],
        out_specs=(vmem, vmem, vmem, vmem),
        scratch_shapes=[
            pltpu.VMEM((n, rows, width), BF16),
            pltpu.VMEM(logits.shape, BF16),
            pltpu.VMEM((kvb, width), BF16),
            pltpu.VMEM((kvb, width), BF16),
            pltpu.VMEM((n, k, rows, kvb), BF16),
            pltpu.VMEM((rows, 128), F32),
            pltpu.VMEM((k, 8, rows), F32),
            pltpu.VMEM((n, 8, rows), F32),
            pltpu.VMEM((n, n, 1, rows), F32),
            pltpu.VMEM((n, 1, width), F32),
            dma((3,)),
            dma((2, n // 2 + 1, 2)),
            dma((2, n // 2 + 1, 2)),
            dma((k,)),
            dma,
            dma((n, k)),
            dma((n, k)),
            dma((k,)),
            dma((k,)),
            dma((n,)),
            dma((n,)),
            dma((n,)),
            dma((n,)),
            dma((n,)),
            dma((n,)),
        ],
        compiler_params=pltpu.CompilerParams(
            collective_id=0, has_side_effects=True, vmem_limit_bytes=58 << 20
        ),
        cost_estimate=pl.CostEstimate(
            flops=4 * n * rows * width * kvb, bytes_accessed=16 << 20, transcendentals=rows * 8000
        ),
    )(
        hidden, target_weight, draft_weight, logits,
        draft_gain.reshape(1, -1), target_gain.reshape(1, -1), info,
    )
    grad_weight = gw * draft_gain[None, :]
    mine = lax.axis_index("dp").astype(F32)
    member = messages[:, 1, :] == mine
    before = (index[:, None] <= index[None, :]).astype(BF16)
    running = jnp.dot(member.astype(BF16), before, preferred_element_type=F32)
    slots = jnp.arange(1, capacity + 1, dtype=jnp.int32).astype(F32)
    chosen = jnp.logical_and(running[:, None, :] == slots[None, :, None], member[:, None, :])
    slot_loss = jnp.sum(jnp.where(chosen, loss, 0.0), axis=2).reshape(n * capacity)
    return (grad_weight, gain.reshape(width), slot_loss)


def solution(mesh):
    in_specs = (
        P("dp", "mp"), P(), P("mp", None), P("mp"), P("dp", "mp"),
        P("dp", "mp"), P("dp", None), P("dp"), P("dp", None),
    )
    out_specs = (P("dp", "mp"), P("mp"), P("dp"))
    return jax.shard_map(
        on_device, mesh=mesh, in_specs=in_specs, out_specs=out_specs, check_vma=False
    )
```

time: 546 us -> 121 us (0.22)
  waiting for transfers between devices: 433 us -> 0 us
  Pallas kernels: 0 us -> 107 us
  blocking collectives: 47.9 us -> 0 us
  matrix products: 29.8 us -> 0.15 us
  between operations: 13.9 us -> 0.7 us
  other arithmetic: 12.6 us -> 4.97 us
  starting transfers between devices: 5.89 us -> 0 us
  local copies, waits for them, and re-layouts: 2.69 us -> 8.44 us
    reduce_scatter x1 -> x0, waiting for transfers between devices: 243 us -> none  [on_device(): lax.psum_scatter(lax.dot_general(grad_out, normed, (((0,), (0,)), ((), ()...]
    all_gather x3 -> x0, waiting for transfers between devices: 134 us -> none  [the longest x1 96.1 us: on_device(): full_weight = lax.all_gather(draft_weight, 'dp', axis=0, tiled=True)]
    pallas_call x0 -> x1, Pallas kernels: none -> 107 us  [on_device(): pl.pallas_call(functools.partial(kernel, n, k), out_shape=(jax.ShapeDtype...]
    psum x1 -> x0, waiting for transfers between devices: 54.2 us -> none  [on_device(): projection = lax.psum(partial_value, 'mp')]
    psum x2 -> x0, blocking collectives: 32.7 us -> none  [the longest x1 24.3 us: on_device(): grad_gain = lax.psum(gain_local, 'dp')]
    dot_general x5 -> x1, matrix products: 29.8 us -> 0.15 us  [on_device(): running = jnp.dot(member.astype(BF16), before, preferred_element_type=F32)]
    all_gather x3 -> x0, blocking collectives: 15.2 us -> none  [joined(): everything = jax.tree.map(lambda part: lax.all_gather(part, axis), shard)]
    unnamed x25 -> x14, local copies, waits for them, and re-layouts: 0.84 us -> 7.78 us
  transfers between devices with their start and end apart: 6 -> 0, of which waited for: 5 -> 0; matrix products, arithmetic and copies ran while one was open for 6% -> 0% of each run, Pallas kernels for 0% -> 0%
where the time goes in v1:
time: 121 us
  Pallas kernels  107 us (88%)
  local copies, waits for them, and re-layouts  8.44 us (7%)
  other arithmetic  4.97 us (4%)
    pallas_call x1, Pallas kernels, on_device(): pl.pallas_call(functools.partial(kernel, n, k), out_shape=(jax.ShapeDtype...  107 us
    unnamed x14, local copies, waits for them, and re-layouts  7.78 us
    mul x1, other arithmetic, on_device(): grad_weight = gw * draft_gain[None, :]  3.22 us

profile of v1, /device:TPU:0, one launch (start us, length us, event | category | flops | bytes accessed | tf_op | source)
XLA Modules:
  0.0 121.0 jit_solution(2328830217186801918)
XLA Ops:
  0.6 0.0 copy-start.4
  0.6 0.0 copy-start.2
  0.7 0.0 copy-start.3
  0.7 6.4 %copy.14.logits = bf16[256,8000]{1,0:T(8,128)(2,1)} copy(bf16[256,8000]{0,1:T(8,128)(2,1)} %param.14) | data formatting | bytes 8192000 | tf_op args[5]
  7.1 0.0 copy-done.4
  7.1 0.1 fusion.1
  7.2 0.0 copy-done.2
  7.2 0.0 copy-done.3
  7.2 0.6 pad_maximum_fusion.info
  7.8 0.0 copy-start
  7.8 106.7 %shard_map.112 = (f32[256,2048]{1,0:T(8,128)}, f32[1,2048]{1,0:T(1,128)}, f32[8,1,256]{2,1,0:T(1,128)}, f32[8,8,256]{2,1,0:T(8,128)}) custom-call(bf16[256,2048]{1,0:T(8,128)(2,1)} %hidden.1, bf16[512,8192]{1,0:T(8,128)(2,1)} %tw.1, bf16[256,2048]{1,0:T(8,128)(2,1)} %dw.1, bf16[256,8000]{1,0:T(8,128)(2,1)} %copy.14.logits, f32[1,2048]{1,0:T(1,128)} %bitcast.15, ...), custom_call_target="tpu_custom_call" | custom-call | flops 4294967296 | bytes 16777216 | tf_op jit(solution)/shard_map/pallas_call | solution.py:339
  114.5 0.9 slice_compare_fusion
  115.4 0.1 fusion
  115.5 0.7 copy.19
  116.3 0.2 select_reduce_fusion
  116.5 0.7 reshape.54
  117.1 0.0 copy-done
  117.1 0.0 copy-start.1
  117.1 3.2 %broadcast_multiply_fusion = f32[256,2048]{1,0:T(8,128)} fusion(f32[256,2048]{1,0:T(8,128)} %get-tuple-element.7, f32[2048]{0:T(1024)S(1)} %copy-done), kind=kLoop, calls=%fused_computation | loop fusion | flops 524288 | bytes 4202496 | tf_op jit(solution)/shard_map/mul | solution.py:386
  120.4 0.0 copy-done.1
  120.4 0.6 copy.22
  (5 shorter events, 0.0 us)
Async XLA Ops:
  0.6 6.5 %copy-start.4 = (s32[1,2]{1,0:T(1,128)S(1)}, s32[1,2]{1,0:T(1,128)}, u32[]{:S(2)}) copy-start(s32[1,2]{1,0:T(1,128)} %param.15) | copy-start | bytes 28
  0.6 6.6 %copy-start.2 = (s32[256]{0:T(256)S(1)}, s32[256]{0:T(256)}, u32[]{:S(2)}) copy-start(s32[256]{0:T(256)} %param.16) | copy-start | bytes 3076
  0.7 6.6 %copy-start.3 = (s32[256,1]{0,1:T(1,128)S(1)}, s32[256,1]{0,1:T(1,128)}, u32[]{:S(2)}) copy-start(s32[256,1]{0,1:T(1,128)} %param.17) | copy-start | bytes 3076
  7.8 109.3 %copy-start = (f32[2048]{0:T(1024)S(1)}, f32[2048]{0:T(1024)}, u32[]{:S(2)}) copy-start(f32[2048]{0:T(1024)} %param.12) | copy-start | bytes 24580
  117.1 3.2 %copy-start.1 = (f32[1,2048]{1,0:T(1,128)S(1)}, f32[1,2048]{1,0:T(1,128)}, u32[]{:S(2)}) copy-start(f32[1,2048]{1,0:T(1,128)} %get-tuple-element.8) | copy-start | bytes 24580

commit v2 on v1

v2 whole, which is shorter than its diff:
```python
import functools
import math

import jax
import jax.numpy as jnp
from jax import lax
from jax.experimental import pallas as pl
from jax.experimental.pallas import tpu as pltpu
from jax.sharding import PartitionSpec as P

LEN = 128
SEQS = 2
EPSILON = 1e-05
MESH = pl.DeviceIdType.MESH
F32 = jnp.float32
BF16 = jnp.bfloat16


def place_of(index, n):
    odd = lax.rem(index, 2)
    half = lax.div(index, 2)
    return (1 - odd) * half + odd * (n - 1 - half)


def index_of(place, n):
    late = lax.div(place, n // 2)
    return (1 - late) * (2 * place) + late * (2 * (n - 1 - place) + 1)


def kernel(
    n, k, capacity,
    hidden, tw, dweight, logits, gd, gt, info,
    gw, gain_out, slot_out,
    hid, lbuf, twb, dw, wd, sbuf, st, smsg, cmsg, fac, key, qf, gf, totf,
    local_sem, ring_send, ring_recv, tw_send, tw_recv, ex_send, ex_recv,
    st_send, st_recv, c_send, c_recv, q_send, q_recv, g_send, g_recv,
):
    rows, width = hidden.shape
    kvb = dw.shape[0]
    quarter, half = rows // 4, rows // 2
    vocab = logits.shape[0] * k
    d = lax.axis_index("dp")
    m = lax.axis_index("mp")
    place = place_of(d, n)
    right = index_of(lax.rem(place + 1, n), n)
    left = index_of(lax.rem(place + n - 1, n), n)
    holder = lax.div(d * k, n)
    offset = pl.multiple_of(d * kvb - holder * tw.shape[0], 16)

    own_hidden = pltpu.make_async_copy(hidden, hid.at[0], local_sem.at[0])
    own_logits = pltpu.make_async_copy(logits, lbuf, local_sem.at[1])
    own_weight = pltpu.make_async_copy(dweight, dw, local_sem.at[3])

    barrier = pltpu.get_barrier_semaphore()
    for j in range(1, n):
        pl.semaphore_signal(
            barrier, inc=1, device_id={"dp": lax.rem(d + j, n)}, device_id_type=MESH
        )
    for j in range(1, k):
        pl.semaphore_signal(
            barrier, inc=1, device_id={"mp": lax.rem(m + j, k)}, device_id_type=MESH
        )
    own_hidden.start()
    own_logits.start()
    own_weight.start()
    pl.semaphore_wait(barrier, n - 1 + k - 1)

    def ring(way, t, q, first=False):
        part = pl.ds(q * quarter, quarter)
        if way == 0:
            source, target, to = t - 1, t, right
        else:
            source, target, to = lax.rem(n - t + 1, n), n - t, left
        return pltpu.make_async_remote_copy(
            src_ref=hidden.at[part] if first else hid.at[source, part],
            dst_ref=hid.at[target, part],
            send_sem=ring_send.at[way, t, q],
            recv_sem=ring_recv.at[way, t, q],
            device_id={"dp": to},
            device_id_type=MESH,
        )

    def turn(way, i):
        return i if way == 0 else 3 - i

    for i in range(4):
        for way in (0, 1):
            ring(way, 1, turn(way, i), True).start()

    def tw_columns(index):
        return tw.at[pl.ds(offset, kvb), pl.ds(pl.multiple_of(index * width, width), width)]

    def tw_copy(j):
        to = lax.rem(m + j, k)
        return pltpu.make_async_remote_copy(
            src_ref=tw_columns(to), dst_ref=twb,
            send_sem=tw_send.at[j], recv_sem=tw_recv,
            device_id={"mp": to}, device_id_type=MESH,
        )

    tw_own = pltpu.make_async_copy(tw_columns(m), twb, local_sem.at[2])

    @pl.when(m == holder)
    def _():
        for j in range(1, k):
            tw_copy(j).start()
        tw_own.start()

    own_hidden.wait()
    own_logits.wait()
    own_weight.wait()
    entries = logits.shape[0]
    chunk = max(c for c in range(8, 168, 8) if entries % c == 0)

    def folded(values, combine):
        return combine(values.reshape(chunk // 8, 8, rows), axis=0)

    def entries_of(i):
        return lbuf[pl.ds(pl.multiple_of(i * chunk, chunk), chunk), :].astype(F32)

    def largest(i, so_far):
        return jnp.maximum(so_far, folded(entries_of(i), jnp.max))

    highest = lax.fori_loop(
        0, entries // chunk, largest, jnp.full((8, rows), -jnp.inf, F32)
    )
    highest = jnp.max(highest, axis=0, keepdims=True)

    def sums(i, carry):
        shifted = entries_of(i) - highest
        expsum = jnp.exp(shifted)
        return carry[0] + folded(expsum, jnp.sum), carry[1] + folded(expsum * shifted, jnp.sum)

    zero = jnp.zeros((8, rows), F32)
    total, moment = lax.fori_loop(0, entries // chunk, sums, (zero, zero))
    total = jnp.sum(total, axis=0, keepdims=True)
    moment = jnp.sum(moment, axis=0, keepdims=True)

    def row_squares(i, carry):
        r = pl.ds(pl.multiple_of(i * 16, 16), 16)
        features = hid[0, r, :].astype(F32)
        features = features * features
        part = features[:, 0:128]
        for c in range(128, width, 128):
            part += features[:, c:c + 128]
        st[r, :] = part
        return carry

    lax.fori_loop(0, rows // 16, row_squares, 0)
    squares = jnp.sum(st[...].T, axis=0, keepdims=True)
    line = lax.broadcasted_iota(jnp.int32, (8, rows), 0)
    smsg[m] = jnp.where(
        line == 0, highest, jnp.where(line == 1, total, jnp.where(line == 2, moment, squares))
    )

    def st_copy(j):
        return pltpu.make_async_remote_copy(
            src_ref=smsg.at[m], dst_ref=smsg.at[m],
            send_sem=st_send.at[j], recv_sem=st_recv.at[j],
            device_id={"mp": lax.rem(m + j, k)}, device_id_type=MESH,
        )

    for j in range(1, k):
        st_copy(j).start()
    gw[...] = jnp.zeros_like(gw)
    for j in range(1, k):
        st_copy(j).wait()
    highest = smsg[0, 0:1, :]
    for j in range(1, k):
        highest = jnp.maximum(highest, smsg[j, 0:1, :])
    total = jnp.zeros_like(highest)
    moment = jnp.zeros_like(highest)
    squares = jnp.zeros_like(highest)
    for j in range(k):
        below = smsg[j, 0:1, :] - highest
        factor = jnp.exp(below)
        total += factor * smsg[j, 1:2, :]
        moment += factor * (smsg[j, 2:3, :] + below * smsg[j, 1:2, :])
        squares += smsg[j, 3:4, :]
    inverse = lax.rsqrt(squares / (width * k) + EPSILON)
    entropy = jnp.log(total) - moment / total
    weight = (info[0:1, :] * entropy / math.log(vocab)).astype(BF16).astype(F32)
    factor = weight * inverse * inverse * (1.0 / math.sqrt(rows * n))
    cmsg[d] = jnp.where(line == 0, factor, info[1:2, :])

    def c_copy(j):
        return pltpu.make_async_remote_copy(
            src_ref=cmsg.at[d], dst_ref=cmsg.at[d],
            send_sem=c_send.at[j], recv_sem=c_recv.at[j],
            device_id={"dp": lax.rem(d + j, n)}, device_id_type=MESH,
        )

    for j in range(1, n):
        c_copy(j).start()

    def arrive(t, i, onward=True):
        for way in (0, 1):
            ring(way, t, turn(way, i)).wait_recv()
            if onward and i < 2:
                ring(way, t + 1, turn(way, i)).start()
            elif onward:
                @pl.when(t + 1 < n // 2)
                def _():
                    ring(way, t + 1, turn(way, i)).start()

    for i in range(4):
        arrive(1, i)

    for j in range(1, n):
        c_copy(j).wait()

    def columns(s, carry):
        block = index_of(lax.rem(place - s + n, n), n)
        fac[s] = jnp.broadcast_to(cmsg[block][0:1, :], (128, rows)).T
        return carry

    lax.fori_loop(0, n, columns, 0)
    mine = (lax.broadcasted_iota(jnp.int32, (1, rows), 1) * 0 + d).astype(F32)
    before = (
        lax.broadcasted_iota(jnp.int32, (rows, rows), 0)
        <= lax.broadcasted_iota(jnp.int32, (rows, rows), 1)
    ).astype(F32).astype(BF16)

    def slots(j, carry):
        member = jnp.where(cmsg[j] == mine, 1.0, 0.0)
        member = jnp.where(line == 1, member, 0.0)
        running = jnp.dot(member.astype(BF16), before, preferred_element_type=F32)
        key[j] = (running * member)[1:2, :]
        return carry

    lax.fori_loop(0, n, slots, 0)

    @pl.when(m == holder)
    def _():
        tw_own.wait()
        for j in range(1, k):
            tw_copy(j).wait_send()

    @pl.when(m != holder)
    def _():
        tw_copy(1).wait_recv()

    gt_part = gt[:, pl.ds(pl.multiple_of(m * width, width), width)]

    def blend(i, carry):
        r = pl.ds(pl.multiple_of(i * 16, 16), 16)
        wd[r, :] = (
            gd[...] * dw[r, :].astype(F32) - gt_part * twb[r, :].astype(F32)
        ).astype(BF16)
        return carry

    lax.fori_loop(0, kvb // 16, blend, 0)

    def exchange(s, p, start, size, j):
        spot = sbuf.at[s, m, pl.ds(start, size)]
        return pltpu.make_async_remote_copy(
            src_ref=spot, dst_ref=spot,
            send_sem=ex_send.at[s, p, j], recv_sem=ex_recv.at[s, p, j],
            device_id={"mp": lax.rem(m + j, k)}, device_id_type=MESH,
        )

    def project(s, p, start, size):
        sbuf[s, m, start:start + size, :] = lax.dot_general(
            hid[s, start:start + size, :], wd[...], (((1,), (1,)), ((), ())),
            preferred_element_type=F32,
        ).astype(BF16)
        for j in range(1, k):
            exchange(s, p, start, size, j).start()

    piece = min(width, 512)
    ones = jnp.ones((16, kvb), BF16)

    def line_sums(total):
        square = total * total
        high = square.astype(BF16)
        low = (square - high.astype(F32)).astype(BF16)
        over = (((1,), (1,)), ((), ()))
        return (
            lax.dot_general(ones, high, over, preferred_element_type=F32)
            + lax.dot_general(ones, low, over, preferred_element_type=F32)
        )[0:1, :]

    def consume(parts, last=False):
        grads = []
        for s, p, start, size in parts:
            for j in range(1, k):
                exchange(s, p, start, size, j).wait()
            total = sbuf[s, 0, start:start + size, :].astype(F32)
            for j in range(1, k):
                total += sbuf[s, j, start:start + size, :].astype(F32)
            grads.append((total * fac[s, start:start + size, 0:1]).astype(BF16))
            if last:
                totf[start:start + size, :] = total
            else:
                block = index_of(lax.rem(place - s + n, n), n)
                qf[d, block, :, start:start + size] = line_sums(total)
        for c in range(0, width, piece):
            more = gw[:, c:c + piece]
            for (s, p, start, size), grad in zip(parts, grads):
                more += lax.dot_general(
                    grad, hid[s, start:start + size, c:c + piece], (((0,), (0,)), ((), ())),
                    preferred_element_type=F32,
                )
            gw[:, c:c + piece] = more

    def unit(t, u):
        return [(t, u, u * half, half), (n - t, 1 - u, (1 - u) * half, half)]

    def own():
        return [(0, 0, 0, half), (0, 1, half, half)]

    for part in own() + unit(1, 0) + unit(1, 1):
        project(*part)
    consume(own())

    def step(t, carry):
        for u in (0, 1):
            arrive(t, 2 * u)
            arrive(t, 2 * u + 1)
            for part in unit(t, u):
                project(*part)
            consume(unit(t - 1, u))
        return carry

    lax.fori_loop(2, n // 2, step, 0)
    far = n // 2
    outer = [(far, 0, 0, quarter), (far, 1, rows - quarter, quarter)]
    inner = [(far, 2, quarter, half)]
    consume(unit(far - 1, 0))
    arrive(far, 0, False)
    for part in outer:
        project(*part)
    consume(unit(far - 1, 1))
    arrive(far, 1, False)
    for part in inner:
        project(*part)
    consume(outer, True)

    def sent(t, carry):
        for way in (0, 1):
            for i in (0, 1):
                ring(way, t, turn(way, i)).wait_send()

            @pl.when(t < n // 2)
            def _():
                for i in (2, 3):
                    ring(way, t, turn(way, i)).wait_send()

        return carry

    for way in (0, 1):
        for i in range(4):
            ring(way, 1, i, True).wait_send()
    lax.fori_loop(2, n // 2 + 1, sent, 0)
    consume(inner, True)
    qf[d, index_of(lax.rem(place - far + n, n), n)] = line_sums(totf[...])

    def q_copy(j):
        return pltpu.make_async_remote_copy(
            src_ref=qf.at[d], dst_ref=qf.at[d],
            send_sem=q_send.at[j], recv_sem=q_recv.at[j],
            device_id={"dp": lax.rem(d + j, n)}, device_id_type=MESH,
        )

    def g_copy(j):
        return pltpu.make_async_remote_copy(
            src_ref=gf.at[d], dst_ref=gf.at[d],
            send_sem=g_send.at[j], recv_sem=g_recv.at[j],
            device_id={"dp": lax.rem(d + j, n)}, device_id_type=MESH,
        )

    for j in range(1, n):
        q_copy(j).start()
    for c in range(0, width, piece):
        gf[d, :, c:c + piece] = jnp.sum(
            dw[:, c:c + piece].astype(F32) * gw[:, c:c + piece], axis=0, keepdims=True
        )
    for j in range(1, n):
        g_copy(j).start()
    for j in range(1, n):
        q_copy(j).wait()
    loss = qf[0]
    for j in range(1, n):
        loss += qf[j]
    number = (lax.broadcasted_iota(jnp.int32, (capacity, rows), 0) + 1).astype(F32)
    column = lax.broadcasted_iota(jnp.int32, (capacity, 128), 1)
    gathered = jnp.zeros((capacity, 128), F32)
    for j in range(n):
        worth = loss[j] * (0.5 * cmsg[j, 0:1, :])
        held = jnp.sum(jnp.where(number == key[j], worth, 0.0), axis=1, keepdims=True)
        gathered = jnp.where(column == j, held, gathered)
    slot_out[...] = jnp.concatenate(
        [gathered, jnp.zeros((128 - capacity, 128), F32)], axis=0
    ).T[0:n, :]
    for j in range(1, n):
        g_copy(j).wait()
    gain = gf[0]
    for j in range(1, n):
        gain += gf[j]
    gain_out[...] = gain


def on_device(
    hidden, target_gain, target_weight, draft_gain, draft_weight, logits, seq_lens, tool_mask, owners
):
    n = lax.axis_size("dp")
    k = lax.axis_size("mp")
    rows, width = hidden.shape
    kvb = draft_weight.shape[0]
    capacity = max(2, 5 * rows // (4 * n))
    whole_tiles = -(-capacity // 8) * 8
    index = jnp.arange(rows, dtype=jnp.int32)
    position = index % LEN
    lookup = (index // LEN)[:, None] == jnp.arange(SEQS, dtype=jnp.int32)[None, :]
    length = jnp.sum(jnp.where(lookup, seq_lens[0][None, :], 0), axis=1)
    valid = jnp.logical_and(position < length - 1, tool_mask == 1).astype(F32)
    info = jnp.stack([valid, owners[:, 0].astype(F32)])
    anywhere = pl.BlockSpec(memory_space=pl.ANY)
    vmem = pl.BlockSpec(memory_space=pltpu.VMEM)
    dma = pltpu.SemaphoreType.DMA
    gw, gain, slots = pl.pallas_call(
        functools.partial(kernel, n, k, whole_tiles),
        out_shape=(
            jax.ShapeDtypeStruct((kvb, width), F32),
            jax.ShapeDtypeStruct((1, width), F32),
            jax.ShapeDtypeStruct((n, 128), F32),
        ),
        in_specs=[anywhere, anywhere, anywhere, anywhere, vmem, vmem, vmem],
        out_specs=(vmem, vmem, vmem),
        scratch_shapes=[
            pltpu.VMEM((n, rows, width), BF16),
            pltpu.VMEM((logits.shape[1], rows), BF16),
            pltpu.VMEM((kvb, width), BF16),
            pltpu.VMEM((kvb, width), BF16),
            pltpu.VMEM((kvb, width), BF16),
            pltpu.VMEM((n, k, rows, kvb), BF16),
            pltpu.VMEM((rows, 128), F32),
            pltpu.VMEM((k, 8, rows), F32),
            pltpu.VMEM((n, 8, rows), F32),
            pltpu.VMEM((n, rows, 128), F32),
            pltpu.VMEM((n, 1, rows), F32),
            pltpu.VMEM((n, n, 1, rows), F32),
            pltpu.VMEM((n, 1, width), F32),
            pltpu.VMEM((rows, kvb), F32),
            dma((4,)),
            dma((2, n // 2 + 1, 4)),
            dma((2, n // 2 + 1, 4)),
            dma((k,)),
            dma,
            dma((n, 3, k)),
            dma((n, 3, k)),
            dma((k,)),
            dma((k,)),
            dma((n,)),
            dma((n,)),
            dma((n,)),
            dma((n,)),
            dma((n,)),
            dma((n,)),
        ],
        compiler_params=pltpu.CompilerParams(
            collective_id=0, has_side_effects=True, vmem_limit_bytes=58 << 20
        ),
        cost_estimate=pl.CostEstimate(
            flops=4 * n * rows * width * kvb,
            bytes_accessed=2 * (logits.size + 4 * kvb * width),
            transcendentals=logits.size,
        ),
    )(
        hidden, target_weight, draft_weight, logits.T,
        draft_gain.reshape(1, -1), target_gain.reshape(1, -1), info,
    )
    grad_weight = gw * draft_gain[None, :]
    return (grad_weight, gain.reshape(width), slots[:, 0:capacity].reshape(n * capacity))


def solution(mesh):
    in_specs = (
        P("dp", "mp"), P(), P("mp", None), P("mp"), P("dp", "mp"),
        P("dp", "mp"), P("dp", None), P("dp"), P("dp", None),
    )
    out_specs = (P("dp", "mp"), P("mp"), P("dp"))
    return jax.shard_map(
        on_device, mesh=mesh, in_specs=in_specs, out_specs=out_specs, check_vma=False
    )
```

time: 121 us -> 112 us (0.926)
  local copies, waits for them, and re-layouts: 8.44 us -> 1.27 us
  Pallas kernels: 107 us -> 104 us
    unnamed x14 -> x7, local copies, waits for them, and re-layouts: 7.78 us -> 0.61 us
    pallas_call x1, Pallas kernels: 107 us -> 104 us  [on_device(): pl.pallas_call(functools.partial(kernel, n, k, whole_tiles), out_shape=(j...]
where the time goes in v2:
time: 112 us
  Pallas kernels  104 us (93%)
  other arithmetic  5.91 us (5%)
  local copies, waits for them, and re-layouts  1.27 us (1%)
    pallas_call x1, Pallas kernels, on_device(): pl.pallas_call(functools.partial(kernel, n, k, whole_tiles), out_shape=(j...  104 us
    mul x1, other arithmetic, on_device(): grad_weight = gw * draft_gain[None, :]  3.21 us

profile of v2, /device:TPU:0, one launch (start us, length us, event | category | flops | bytes accessed | tf_op | source)
XLA Modules:
  0.0 112.2 jit_solution(6774325407820712085)
XLA Ops:
  0.6 0.7 convert_bitcast_fusion
  1.3 0.7 fusion
  2.1 0.7 and_convert_fusion
  2.7 0.6 pad_maximum_fusion.info
  3.3 0.0 copy-start
  3.3 104.3 %shard_map.112 = (f32[256,2048]{1,0:T(8,128)}, f32[1,2048]{1,0:T(1,128)}, f32[8,128]{1,0:T(8,128)}) custom-call(bf16[256,2048]{1,0:T(8,128)(2,1)} %hidden.1, bf16[512,8192]{1,0:T(8,128)(2,1)} %tw.1, bf16[256,2048]{1,0:T(8,128)(2,1)} %dweight.1, bf16[8000,256]{1,0:T(8,128)(2,1)} %bitcast.14, f32[1,2048]{1,0:T(1,128)} %bitcast.9, f32[1,8192]{1,0:T(1,128)} %bitcast.15, ...), custom_call_target="tpu_custom_call" | custom-call | flops 4294967296 | bytes 8290304 | tf_op jit(solution)/shard_map/pallas_call | solution.py:421
  107.7 0.0 copy-done
  107.7 0.0 copy-start.2
  107.7 0.0 copy-start.1
  107.7 3.2 %broadcast_multiply_fusion = f32[256,2048]{1,0:T(8,128)} fusion(f32[256,2048]{1,0:T(8,128)} %get-tuple-element.6, f32[2048]{0:T(1024)S(1)} %copy-done), kind=kLoop, calls=%fused_computation | loop fusion | flops 524288 | bytes 4202496 | tf_op jit(solution)/shard_map/mul | solution.py:473
  110.9 0.0 copy-done.2
  110.9 0.7 reshape.46
  111.6 0.0 copy-done.1
  111.6 0.6 copy.13
  (1 shorter events, 0.0 us)
Async XLA Ops:
  3.3 104.4 %copy-start = (f32[2048]{0:T(1024)S(1)}, f32[2048]{0:T(1024)}, u32[]{:S(2)}) copy-start(f32[2048]{0:T(1024)} %param.12) | copy-start | bytes 24580
  107.7 3.2 %copy-start.2 = (f32[8,128]{1,0:T(8,128)S(1)}, f32[8,128]{1,0:T(8,128)}, u32[]{:S(2)}) copy-start(f32[8,128]{1,0:T(8,128)} %get-tuple-element.8) | copy-start | bytes 12292
  107.7 3.9 %copy-start.1 = (f32[1,2048]{1,0:T(1,128)S(1)}, f32[1,2048]{1,0:T(1,128)}, u32[]{:S(2)}) copy-start(f32[1,2048]{1,0:T(1,128)} %get-tuple-element.7) | copy-start | bytes 24580

commit v3 on v2

--- a/solution.py
+++ b/solution.py
@@ -29,11 +29,11 @@
 
 def kernel(
     n, k, capacity,
-    hidden, tw, dweight, logits, gd, gt, info,
-    gw, gain_out, slot_out,
-    hid, lbuf, twb, dw, wd, sbuf, st, smsg, cmsg, fac, key, qf, gf, totf,
+    hidden, tw, dweight, logits, gd, gt, lens, mask, owner,
+    gw_out, gain_out, slot_out,
+    hid, lbuf, twb, dw, wd, sbuf, st, smsg, cmsg, fac, key, qf, gf, totf, gw,
     local_sem, ring_send, ring_recv, tw_send, tw_recv, ex_send, ex_recv,
-    st_send, st_recv, c_send, c_recv, q_send, q_recv, g_send, g_recv,
+    st_send, st_recv, c_send, c_recv, q_send, q_recv, g_send, g_recv, out_sem,
 ):
     rows, width = hidden.shape
     kvb = dw.shape[0]
@@ -163,6 +163,7 @@
     for j in range(1, k):
         st_copy(j).start()
     gw[...] = jnp.zeros_like(gw)
+    qf[d] = jnp.zeros((n, 1, rows), F32)
     for j in range(1, k):
         st_copy(j).wait()
     highest = smsg[0, 0:1, :]
@@ -179,9 +180,16 @@
         squares += smsg[j, 3:4, :]
     inverse = lax.rsqrt(squares / (width * k) + EPSILON)
     entropy = jnp.log(total) - moment / total
-    weight = (info[0:1, :] * entropy / math.log(vocab)).astype(BF16).astype(F32)
+    index = lax.broadcasted_iota(jnp.int32, (1, rows), 1)
+    length = jnp.zeros((1, rows), jnp.int32)
+    for q in range(rows // LEN):
+        length = jnp.where(index // LEN == q, lens[0:1, q:q + 1], length)
+    valid = jnp.where(
+        jnp.logical_and(index % LEN < length - 1, mask[...] == 1), 1.0, 0.0
+    )
+    weight = (valid * entropy / math.log(vocab)).astype(BF16).astype(F32)
     factor = weight * inverse * inverse * (1.0 / math.sqrt(rows * n))
-    cmsg[d] = jnp.where(line == 0, factor, info[1:2, :])
+    cmsg[d] = jnp.where(line == 0, factor, owner[...].astype(F32))
 
     def c_copy(j):
         return pltpu.make_async_remote_copy(
@@ -280,7 +288,13 @@
             + lax.dot_general(ones, low, over, preferred_element_type=F32)
         )[0:1, :]
 
-    def consume(parts, last=False):
+    def write_out(c):
+        columns_of = pl.ds(c, piece)
+        return pltpu.make_async_copy(
+            gw.at[:, columns_of], gw_out.at[:, columns_of], out_sem.at[c // piece]
+        )
+
+    def consume(parts, last=False, final=False):
         grads = []
         for s, p, start, size in parts:
             for j in range(1, k):
@@ -302,6 +316,11 @@
                     preferred_element_type=F32,
                 )
             gw[:, c:c + piece] = more
+            if final:
+                write_out(c).start()
+                gf[d, :, c:c + piece] = jnp.sum(
+                    dw[:, c:c + piece].astype(F32) * more, axis=0, keepdims=True
+                )
 
     def unit(t, u):
         return [(t, u, u * half, half), (n - t, 1 - u, (1 - u) * half, half)]
@@ -334,6 +353,16 @@
     arrive(far, 1, False)
     for part in inner:
         project(*part)
+
+    def q_copy(j):
+        return pltpu.make_async_remote_copy(
+            src_ref=qf.at[d], dst_ref=qf.at[d],
+            send_sem=q_send.at[j], recv_sem=q_recv.at[j],
+            device_id={"dp": lax.rem(d + j, n)}, device_id_type=MESH,
+        )
+
+    for j in range(1, n):
+        q_copy(j).start()
     consume(outer, True)
 
     def sent(t, carry):
@@ -352,15 +381,8 @@
         for i in range(4):
             ring(way, 1, i, True).wait_send()
     lax.fori_loop(2, n // 2 + 1, sent, 0)
-    consume(inner, True)
-    qf[d, index_of(lax.rem(place - far + n, n), n)] = line_sums(totf[...])
-
-    def q_copy(j):
-        return pltpu.make_async_remote_copy(
-            src_ref=qf.at[d], dst_ref=qf.at[d],
-            send_sem=q_send.at[j], recv_sem=q_recv.at[j],
-            device_id={"dp": lax.rem(d + j, n)}, device_id_type=MESH,
-        )
+    consume(inner, True, True)
+    gf[d, :, width:width + rows] = line_sums(totf[...])
 
     def g_copy(j):
         return pltpu.make_async_remote_copy(
@@ -370,18 +392,26 @@
         )
 
     for j in range(1, n):
-        q_copy(j).start()
-    for c in range(0, width, piece):
-        gf[d, :, c:c + piece] = jnp.sum(
-            dw[:, c:c + piece].astype(F32) * gw[:, c:c + piece], axis=0, keepdims=True
-        )
-    for j in range(1, n):
         g_copy(j).start()
     for j in range(1, n):
         q_copy(j).wait()
-    loss = qf[0]
-    for j in range(1, n):
-        loss += qf[j]
+        g_copy(j).wait()
+    gain = gf[0, :, 0:width]
+    for j in range(1, n):
+        gain += gf[j, :, 0:width]
+    gain_out[...] = gain
+
+    def far_of(j):
+        spot = (j // 2 if j % 2 == 0 else n - 1 - j // 2) - n // 2
+        spot = (spot + n) % n
+        return 2 * spot if spot < n // 2 else 2 * (n - 1 - spot) + 1
+
+    loss = []
+    for b in range(n):
+        lot = jnp.zeros((1, rows), F32)
+        for j in range(n):
+            lot += gf[j, :, width:width + rows] if far_of(j) == b else qf[j, b]
+        loss.append(lot)
     number = (lax.broadcasted_iota(jnp.int32, (capacity, rows), 0) + 1).astype(F32)
     column = lax.broadcasted_iota(jnp.int32, (capacity, 128), 1)
     gathered = jnp.zeros((capacity, 128), F32)
@@ -392,12 +422,8 @@
     slot_out[...] = jnp.concatenate(
         [gathered, jnp.zeros((128 - capacity, 128), F32)], axis=0
     ).T[0:n, :]
-    for j in range(1, n):
-        g_copy(j).wait()
-    gain = gf[0]
-    for j in range(1, n):
-        gain += gf[j]
-    gain_out[...] = gain
+    for c in range(0, width, piece):
+        write_out(c).wait()
 
 
 def on_device(
@@ -409,12 +435,9 @@
     kvb = draft_weight.shape[0]
     capacity = max(2, 5 * rows // (4 * n))
     whole_tiles = -(-capacity // 8) * 8
-    index = jnp.arange(rows, dtype=jnp.int32)
-    position = index % LEN
-    lookup = (index // LEN)[:, None] == jnp.arange(SEQS, dtype=jnp.int32)[None, :]
-    length = jnp.sum(jnp.where(lookup, seq_lens[0][None, :], 0), axis=1)
-    valid = jnp.logical_and(position < length - 1, tool_mask == 1).astype(F32)
-    info = jnp.stack([valid, owners[:, 0].astype(F32)])
+    lanes = -(-kvb // 128) * 128
+    room = 2 * (n * rows * width + logits.size + 3 * kvb * width + n * k * rows * lanes)
+    room += 4 * (n * rows * 128 + kvb * width + rows * lanes) + (6 << 20)
     anywhere = pl.BlockSpec(memory_space=pl.ANY)
     vmem = pl.BlockSpec(memory_space=pltpu.VMEM)
     dma = pltpu.SemaphoreType.DMA
@@ -425,8 +448,8 @@
             jax.ShapeDtypeStruct((1, width), F32),
             jax.ShapeDtypeStruct((n, 128), F32),
         ),
-        in_specs=[anywhere, anywhere, anywhere, anywhere, vmem, vmem, vmem],
-        out_specs=(vmem, vmem, vmem),
+        in_specs=[anywhere] * 4 + [vmem] * 5,
+        out_specs=(anywhere, vmem, vmem),
         scratch_shapes=[
             pltpu.VMEM((n, rows, width), BF16),
             pltpu.VMEM((logits.shape[1], rows), BF16),
@@ -440,8 +463,9 @@
             pltpu.VMEM((n, rows, 128), F32),
             pltpu.VMEM((n, 1, rows), F32),
             pltpu.VMEM((n, n, 1, rows), F32),
-            pltpu.VMEM((n, 1, width), F32),
+            pltpu.VMEM((n, 1, width + rows), F32),
             pltpu.VMEM((rows, kvb), F32),
+            pltpu.VMEM((kvb, width), F32),
             dma((4,)),
             dma((2, n // 2 + 1, 4)),
             dma((2, n // 2 + 1, 4)),
@@ -457,9 +481,10 @@
             dma((n,)),
             dma((n,)),
             dma((n,)),
+            dma((-(-width // 512),)),
         ],
         compiler_params=pltpu.CompilerParams(
-            collective_id=0, has_side_effects=True, vmem_limit_bytes=58 << 20
+            collective_id=0, has_side_effects=True, vmem_limit_bytes=max(room, 58 << 20)
         ),
         cost_estimate=pl.CostEstimate(
             flops=4 * n * rows * width * kvb,
@@ -468,7 +493,8 @@
         ),
     )(
         hidden, target_weight, draft_weight, logits.T,
-        draft_gain.reshape(1, -1), target_gain.reshape(1, -1), info,
+        draft_gain.reshape(1, -1), target_gain.reshape(1, -1),
+        seq_lens, tool_mask.reshape(1, -1), owners.T,
     )
     grad_weight = gw * draft_gain[None, :]
     return (grad_weight, gain.reshape(width), slots[:, 0:capacity].reshape(n * capacity))

time: 112 us -> 109 us (0.973)
  other arithmetic: 5.91 us -> 3.21 us
    another operation x2 -> x0, other arithmetic: 1.27 us -> none  [on_device(): info = jnp.stack([valid, owners[:, 0].astype(F32)])]
where the time goes in v3:
time: 109 us
  Pallas kernels  103 us (94%)
  other arithmetic  3.21 us (3%)
  local copies, waits for them, and re-layouts  1.27 us (1%)
    pallas_call x1, Pallas kernels, on_device(): pl.pallas_call(functools.partial(kernel, n, k, whole_tiles), out_shape=(j...  103 us
    mul x1, other arithmetic, on_device(): grad_weight = gw * draft_gain[None, :]  3.21 us

profile of v3, /device:TPU:0, one launch (start us, length us, event | category | flops | bytes accessed | tf_op | source)
XLA Modules:
  0.0 108.6 jit_solution(6457116405192324888)
XLA Ops:
  0.6 0.0 copy-start
  0.6 103.4 %shard_map.112 = (f32[256,2048]{1,0:T(8,128)}, f32[1,2048]{1,0:T(1,128)}, f32[8,128]{1,0:T(8,128)}) custom-call(bf16[256,2048]{1,0:T(8,128)(2,1)} %hidden.1, bf16[512,8192]{1,0:T(8,128)(2,1)} %tw.1, bf16[256,2048]{1,0:T(8,128)(2,1)} %dweight.1, bf16[8000,256]{1,0:T(8,128)(2,1)} %bitcast.10, f32[1,2048]{1,0:T(1,128)} %bitcast.7, f32[1,8192]{1,0:T(1,128)} %bitcast.11, ...), custom_call_target="tpu_custom_call" | custom-call | flops 4294967296 | bytes 8290304 | tf_op jit(solution)/shard_map/pallas_call | solution.py:444
  104.1 0.0 copy-done
  104.1 0.0 copy-start.2
  104.1 0.0 copy-start.1
  104.1 3.2 %broadcast_multiply_fusion = f32[256,2048]{1,0:T(8,128)} fusion(f32[256,2048]{1,0:T(8,128)} %get-tuple-element.6, f32[2048]{0:T(1024)S(1)} %copy-done), kind=kLoop, calls=%fused_computation | loop fusion | flops 524288 | bytes 4202496 | tf_op jit(solution)/shard_map/mul | solution.py:499
  107.3 0.0 copy-done.2
  107.3 0.7 reshape.26
  108.0 0.0 copy-done.1
  108.0 0.6 copy.13
Async XLA Ops:
  0.6 103.4 %copy-start = (f32[2048]{0:T(1024)S(1)}, f32[2048]{0:T(1024)}, u32[]{:S(2)}) copy-start(f32[2048]{0:T(1024)} %param.12) | copy-start | bytes 24580
  104.1 3.2 %copy-start.2 = (f32[8,128]{1,0:T(8,128)S(1)}, f32[8,128]{1,0:T(8,128)}, u32[]{:S(2)}) copy-start(f32[8,128]{1,0:T(8,128)} %get-tuple-element.8) | copy-start | bytes 12292
  104.1 3.9 %copy-start.1 = (f32[1,2048]{1,0:T(1,128)S(1)}, f32[1,2048]{1,0:T(1,128)}, u32[]{:S(2)}) copy-start(f32[1,2048]{1,0:T(1,128)} %get-tuple-element.7) | copy-start | bytes 24580
